TPU v7x, 128 devices: a whole 4x4x4 slice. The times are simulated.
128 devices in a mesh: row: 8 (over z, core), col: 16 (over x, y).
Axes of the slice: x: 4, y: 4, z: 4, core: 2. Of those that a mesh axis runs over, the one named last changes fastest.
Arguments:
- start_block: float32 [32768, 128], P(('row', 'col')), may hold values from -6 to 6
- degree: float32 [32768], P(('row', 'col')), may hold values from 3.99 to 4.01
- block_values: float32 [49152, 4096], P(('row', 'col')), may hold values from -0.0007324219 to 0.0007324219
- block_rows: int32 [49152], P(('row', 'col')), may hold values from 0 to 31
- block_slots: int32 [49152], P(('row', 'col')), may hold values from 0 to 31, as said below
- need_lists: int32 [2048, 2], P(('row', 'col')), may hold values from 0 to 4, as said below
- live_blocks: int32 [128], P(('row', 'col')), may hold values from 96 to 384, as said below
Outputs:
- alphas: float32 [2, 128, 128], replicated
- betas: float32 [2, 128, 128], replicated
- next_basis: float32 [32768, 128], P(('row', 'col'))
Inputs may be any that keep to these rules, and one draw needn't show every extreme that they name: `need_lists`: entries of a need list are distinct block rows, listed first, then padded with 4; every list has at least one entry, and on every device some list is full with 2 entries. `block_slots`: each slot's value p * 2 + q points at a listed (never padded) entry q of the device's need list p. `live_blocks`: some device uses all 384 slots in every draw.
All inputs are finite; a program needn't handle non-finite values.
Results may differ from a plain program's by a relative error of at most 0.00045.
Values sent between devices are 32-bit elements; how exact they have to be, the bound alone decides.
No kernel may reach another device: no remote copies, remote signals or barrier semaphores. Data moves between devices by JAX's collectives and lax.ppermute only.
A program may use at most 128 MiB of HBM per device.

v0:
```python
import jax
import jax.numpy as jnp
from jax import lax
from jax.sharding import PartitionSpec as P

BS = 64
ITERS = 2
HIGH = lax.Precision.HIGHEST


def local_gram(left, right):
    return jnp.einsum("ra,rb->ab", left, right, precision=HIGH)


def on_device(start_block, degree, block_values, block_rows, block_slots, need_lists, live_blocks):
    row_count = lax.axis_size("row")
    col_count = lax.axis_size("col")
    local_rows, block_width = start_block.shape
    owned_blocks = local_rows // BS
    list_length = need_lists.shape[1]
    capacity = block_values.shape[0]
    group_size = min(128, capacity)
    total_rows = local_rows * row_count * col_count
    live_count = live_blocks[0]
    flat_need = need_lists.reshape(-1)
    stripe_cols = block_slots // list_length * owned_blocks + flat_need[block_slots]
    start_gram = lax.psum(local_gram(start_block, start_block), ("row", "col")) / total_rows
    lower_factor = jnp.linalg.cholesky(start_gram)
    current = lax.linalg.triangular_solve(
        lower_factor, start_block, left_side=False, lower=True, transpose_a=True
    )
    basis_list = [current]
    alpha_list = []
    beta_list = []
    for iteration in range(ITERS):
        owned_rows = current.reshape(owned_blocks, BS, block_width)
        row_side = lax.all_gather(owned_rows, "row", axis=0, tiled=True)
        col_side = lax.all_gather(owned_rows, "col", axis=0, tiled=True)
        col_length = col_count * owned_blocks
        group_total = (live_count + group_size - 1) // group_size

        def group_step(group_index, partials):
            row_part, col_part = partials
            first_slot = group_index * group_size
            values_now = lax.dynamic_slice_in_dim(block_values, first_slot, group_size, 0).reshape(
                group_size, BS, BS
            )
            rows_now = lax.dynamic_slice_in_dim(block_rows, first_slot, group_size, 0)
            cols_now = lax.dynamic_slice_in_dim(stripe_cols, first_slot, group_size, 0)
            in_use = (first_slot + jnp.arange(group_size, dtype=jnp.int32) < live_count).astype(
                current.dtype
            )
            values_now = values_now * in_use[:, None, None]
            forward = jnp.einsum("sab,sbn->san", values_now, col_side[cols_now], precision=HIGH)
            backward = jnp.einsum("sba,sbn->san", values_now, row_side[rows_now], precision=HIGH)
            return (row_part.at[rows_now].add(forward), col_part.at[cols_now].add(backward))

        start_parts = (
            jnp.zeros((row_count * owned_blocks, BS, block_width), current.dtype),
            jnp.zeros((col_length, BS, block_width), current.dtype),
        )
        row_part, col_part = lax.fori_loop(0, group_total, group_step, start_parts)
        row_sum = lax.psum_scatter(row_part, "row", scatter_dimension=0, tiled=True)
        col_sum = lax.psum_scatter(col_part, "col", scatter_dimension=0, tiled=True)
        image_block = degree[:, None] * current - (row_sum + col_sum).reshape(
            local_rows, block_width
        )
        stacked = jnp.concatenate(basis_list, axis=1)
        alpha_block = lax.psum(local_gram(current, image_block), ("row", "col")) / total_rows
        image_block = image_block - jnp.dot(current, alpha_block, precision=HIGH)
        if iteration > 0:
            image_block = image_block - jnp.dot(basis_list[-2], beta_list[-1].T, precision=HIGH)
        projection = lax.psum(local_gram(stacked, image_block), ("row", "col")) / total_rows
        image_block = image_block - jnp.dot(stacked, projection, precision=HIGH)
        norm_gram = lax.psum(local_gram(image_block, image_block), ("row", "col")) / total_rows
        lower_factor = jnp.linalg.cholesky(norm_gram)
        current = lax.linalg.triangular_solve(
            lower_factor, image_block, left_side=False, lower=True, transpose_a=True
        )
        alpha_list.append(alpha_block)
        beta_list.append(lower_factor.T)
        basis_list.append(current)
    return (jnp.stack(alpha_list), jnp.stack(beta_list), current)


def solution(mesh):
    return jax.shard_map(
        on_device,
        mesh=mesh,
        in_specs=(
            P(("row", "col"), None),
            P(("row", "col")),
            P(("row", "col"), None),
            P(("row", "col")),
            P(("row", "col")),
            P(("row", "col"), None),
            P(("row", "col")),
        ),
        out_specs=(P(), P(), P(("row", "col"), None)),
        check_vma=False,
    )
```

profile of v0, /device:TPU:1, one launch (start us, length us, event | category | flops | bytes accessed | tf_op | source)
XLA Modules:
  0.0 1838.1 jit_solution(1668707022313247895)
XLA Ops:
  9.2 145.2 %all-reduce.8.cloned.1.call-done = f32[128,128]{0,1:T(8,128)} async-done(((f32[128,128]{0,1:T(8,128)}), f32[128,128]{0,1:T(8,128)}) %all-reduce.8.cloned.1.call-update) | async-done | bytes 65552 | tf_op jit(solution)/shard_map/psum | solution.py:27
  156.2 11.7 cholesky.59
  189.9 20.1 %fusion.27 = s32[384]{0:T(512)S(1)} fusion(s32[384]{0:T(512)S(1)} %copy-done.16, s32[]{:T(128)} %bitcast.7, s32[]{:T(128)} %bitcast.8, s32[]{:T(128)} %bitcast.9, s32[]{:T(128)} %bitcast.10, s32[]{:T(128)} %bitcast.11, s32[]{:T(128)} %bitcast.12, s32[]{:T(128)} %bitcast.13, s32[]{:T(128)} %bitcast.14, s32[]{:T(128)} %bitcast.15, s32[]{:T(128)} %bitcast.16, ...), kind=kLoop, calls=%fused_computation.85 | loop fusion | flops 31104 | bytes 3200 | tf_op jit(solution)/shard_map/add | solution.py:26
  210.0 37.6 %all-gather.5.cloned.1.call-done = f32[64,64,128]{2,1,0:T(8,128)} async-done(((f32[4,64,128]{2,1,0:T(8,128)}), f32[64,64,128]{2,1,0:T(8,128)}) %all-gather.5.cloned.1.call-update) | async-done | bytes 2097168 | tf_op jit(solution)/shard_map/all_gather | solution.py:38
  249.3 130.8 %while.24 = (s32[]{:T(128)}, f32[32,64,128]{2,1,0:T(8,128)S(1)}, f32[64,64,128]{2,1,0:T(8,128)}, s32[]{:T(128)}, s32[384]{0:T(512)S(1)}, /*index=5*/f32[384,4096...) while((s32[]{:T(128)}, f32[32,64,128]{2,1,0:T(8,128)S(1)}, ...), condition=%wide.region_6.9_spmd, body=%wide.region_3.0_spmd.sunk | while | flops 1613237376 | bytes 96483616 | solution.py:62
  261.2 12.2 fusion.90
  273.4 13.5 scatter_fusion
  299.8 13.5 scatter_fusion.1
  326.4 12.2 fusion.90
  338.5 13.5 scatter_fusion
  364.9 13.5 scatter_fusion.1
  381.8 94.0 %reduce-scatter.5.cloned.1.call-done = f32[4,64,128]{2,1,0:T(8,128)} async-done(((f32[32,64,128]{2,1,0:T(8,128)}), f32[4,64,128]{2,1,0:T(8,128)}) %reduce-scatter.5.cloned.1.call-update) | async-done | bytes 131088 | tf_op jit(solution)/shard_map/reduce_scatter | solution.py:63
  475.7 77.8 %reduce-scatter.7.cloned.1.call-done = f32[4,64,128]{2,1,0:T(8,128)} async-done(((f32[64,64,128]{2,1,0:T(8,128)}), f32[4,64,128]{2,1,0:T(8,128)}) %reduce-scatter.7.cloned.1.call-update) | async-done | bytes 131088 | tf_op jit(solution)/shard_map/reduce_scatter | solution.py:64
  555.6 141.9 %all-reduce.10.cloned.1.call-done = f32[128,128]{0,1:T(8,128)} async-done(((f32[128,128]{0,1:T(8,128)}), f32[128,128]{0,1:T(8,128)}) %all-reduce.10.cloned.1.call-update) | async-done | bytes 65552 | tf_op jit(solution)/shard_map/psum | solution.py:69
  699.6 138.6 %all-reduce.12.cloned.1.call-done = f32[128,128]{0,1:T(8,128)} async-done(((f32[128,128]{0,1:T(8,128)}), f32[128,128]{0,1:T(8,128)}) %all-reduce.12.cloned.1.call-update) | async-done | bytes 65552 | tf_op jit(solution)/shard_map/psum | solution.py:73
  840.4 137.9 %all-reduce.14.cloned.1.call-done = f32[128,128]{0,1:T(8,128)} async-done(((f32[128,128]{0,1:T(8,128)}), f32[128,128]{0,1:T(8,128)}) %all-reduce.14.cloned.1.call-update) | async-done | bytes 65552 | tf_op jit(solution)/shard_map/psum | solution.py:75
  980.0 11.7 cholesky.70
  1005.1 20.4 %all-gather.11.cloned.1.call-done = f32[32,64,128]{2,1,0:T(8,128)} async-done(((f32[4,64,128]{2,1,0:T(8,128)}), f32[32,64,128]{2,1,0:T(8,128)}) %all-gather.11.cloned.1.call-update) | async-done | bytes 1048592 | tf_op jit(solution)/shard_map/all_gather | solution.py:37
  1025.5 46.2 %all-gather.9.cloned.1.call-done = f32[64,64,128]{2,1,0:T(8,128)} async-done(((f32[4,64,128]{2,1,0:T(8,128)}), f32[64,64,128]{2,1,0:T(8,128)}) %all-gather.9.cloned.1.call-update) | async-done | bytes 2097168 | tf_op jit(solution)/shard_map/all_gather | solution.py:38
  1073.5 130.6 %while.25 = (s32[]{:T(128)}, f32[32,64,128]{2,1,0:T(8,128)S(1)}, f32[64,64,128]{2,1,0:T(8,128)}, s32[]{:T(128)}, s32[384]{0:T(512)S(1)}, /*index=5*/f32[384,4096...) while((s32[]{:T(128)}, f32[32,64,128]{2,1,0:T(8,128)S(1)}, ...), condition=%wide.region_15.18_spmd, body=%wide.region_12.0_spmd.sunk | while | flops 1613237376 | bytes 96483616 | solution.py:62
  1085.4 12.2 fusion.96
  1097.6 13.5 scatter_fusion.2
  1123.9 13.5 scatter_fusion.3
  1150.5 12.2 fusion.96
  1162.7 13.5 scatter_fusion.2
  1189.1 13.5 scatter_fusion.3
  1205.7 94.0 %reduce-scatter.9.cloned.1.call-done = f32[4,64,128]{2,1,0:T(8,128)} async-done(((f32[32,64,128]{2,1,0:T(8,128)}), f32[4,64,128]{2,1,0:T(8,128)}) %reduce-scatter.9.cloned.1.call-update) | async-done | bytes 131088 | tf_op jit(solution)/shard_map/reduce_scatter | solution.py:63
  1299.7 77.7 %reduce-scatter.11.cloned.1.call-done = f32[4,64,128]{2,1,0:T(8,128)} async-done(((f32[64,64,128]{2,1,0:T(8,128)}), f32[4,64,128]{2,1,0:T(8,128)}) %reduce-scatter.11.cloned.1.call-update) | async-done | bytes 131088 | tf_op jit(solution)/shard_map/reduce_scatter | solution.py:64
  1379.5 142.1 %all-reduce.16.cloned.1.call-done = f32[128,128]{0,1:T(8,128)} async-done(((f32[128,128]{0,1:T(8,128)}), f32[128,128]{0,1:T(8,128)}) %all-reduce.16.cloned.1.call-update) | async-done | bytes 65552 | tf_op jit(solution)/shard_map/psum | solution.py:69
  1525.6 138.9 %all-reduce.18.cloned.1.call-done = f32[256,128]{1,0:T(8,128)} async-done(((f32[256,128]{1,0:T(8,128)}), f32[256,128]{1,0:T(8,128)}) %all-reduce.18.cloned.1.call-update) | async-done | bytes 131088 | tf_op jit(solution)/shard_map/psum | solution.py:73
  1667.5 137.4 %all-reduce.20.cloned.1.call-done = f32[128,128]{0,1:T(8,128)} async-done(((f32[128,128]{0,1:T(8,128)}), f32[128,128]{0,1:T(8,128)}) %all-reduce.20.cloned.1.call-update) | async-done | bytes 65552 | tf_op jit(solution)/shard_map/psum | solution.py:75
  1806.6 11.7 cholesky.81
  (177 shorter events, 180.3 us)
Async XLA Ops:
  7.2 147.2 %all-reduce.8.cloned.1.call-start = ((), (), s32[]{:S(2)}) async-start(), calls=%async_computation.4 | async-start | bytes 131072 | tf_op jit(solution)/shard_map/psum | solution.py:27
  9.1 200.9 %all-gather.7.cloned.1.call-start = ((), (), s32[]{:S(2)}) async-start(), calls=%async_computation.6 | async-start | bytes 1179648 | tf_op jit(solution)/shard_map/all_gather | solution.py:37
  180.2 67.4 %all-gather.5.cloned.1.call-start = ((), (), s32[]{:S(2)}) async-start(), calls=%async_computation.5 | async-start | bytes 2228224 | tf_op jit(solution)/shard_map/all_gather | solution.py:38
  180.9 294.9 %reduce-scatter.5.cloned.1.call-start = ((), (), s32[]{:S(2)}) async-start(), calls=%async_computation.7 | async-start | bytes 1179648 | tf_op jit(solution)/shard_map/reduce_scatter | solution.py:63
  181.6 6.6 copy-start.17
  181.6 8.3 copy-start.16
  181.6 67.6 %copy-start.15 = (s32[384]{0:T(512)S(1)}, s32[384]{0:T(512)}, u32[]{:S(2)}) copy-start(s32[384]{0:T(512)} %param.17) | copy-start | bytes 4612
  249.3 305.3 %copy-start.14 = (f32[256]{0:T(256)S(1)}, f32[256]{0:T(256)}, u32[]{:S(2)}) copy-start(f32[256]{0:T(256)} %param.15) | copy-start | bytes 3076
  273.4 13.5 copy-start.4
  289.7 10.0 copy-start.8
  338.5 13.5 copy-start.4
  354.9 10.0 copy-start.8
  381.1 172.4 %reduce-scatter.7.cloned.1.call-start = ((), (), s32[]{:S(2)}) async-start(), calls=%async_computation.8 | async-start | bytes 2228224 | tf_op jit(solution)/shard_map/reduce_scatter | solution.py:64
  381.7 315.8 %all-reduce.10.cloned.1.call-start = ((), (), s32[]{:S(2)}) async-start(), calls=%async_computation.9 | async-start | bytes 131072 | tf_op jit(solution)/shard_map/psum | solution.py:69
  555.6 282.7 %all-reduce.12.cloned.1.call-start = ((), (), s32[]{:S(2)}) async-start(), calls=%async_computation.10 | async-start | bytes 131072 | tf_op jit(solution)/shard_map/psum | solution.py:73
  699.6 278.7 %all-reduce.14.cloned.1.call-start = ((), (), s32[]{:S(2)}) async-start(), calls=%async_computation.11 | async-start | bytes 131072 | tf_op jit(solution)/shard_map/psum | solution.py:75
  840.3 185.2 %all-gather.11.cloned.1.call-start = ((), (), s32[]{:S(2)}) async-start(), calls=%async_computation.13 | async-start | bytes 1179648 | tf_op jit(solution)/shard_map/all_gather | solution.py:37
  991.8 33.8 %copy-start.10 = (f32[128,128]{1,0:T(8,128)}, f32[128,128]{1,0:T(8,128)S(1)}, u32[]{:S(2)}) copy-start(f32[128,128]{1,0:T(8,128)S(1)} %cholesky.70) | copy-start | bytes 196612
  1004.5 67.3 %all-gather.9.cloned.1.call-start = ((), (), s32[]{:S(2)}) async-start(), calls=%async_computation.12 | async-start | bytes 2228224 | tf_op jit(solution)/shard_map/all_gather | solution.py:38
  1005.1 294.6 %reduce-scatter.9.cloned.1.call-start = ((), (), s32[]{:S(2)}) async-start(), calls=%async_computation.14 | async-start | bytes 1179648 | tf_op jit(solution)/shard_map/reduce_scatter | solution.py:63
  1097.6 13.5 copy-start.5
  1113.9 10.0 copy-start.6
  1162.7 13.5 copy-start.5
  1179.0 10.0 copy-start.6
  1204.1 175.4 %copy-start.12 = (f32[128,128]{0,1:T(8,128)S(1)}, f32[128,128]{0,1:T(8,128)}, u32[]{:S(2)}) copy-start(f32[128,128]{0,1:T(8,128)} %all-reduce.10.cloned.1.call-done) | copy-start | bytes 196612
  1204.1 318.6 %copy-start.11 = (f32[128,128]{1,0:T(8,128)S(1)}, f32[128,128]{1,0:T(8,128)}, u32[]{:S(2)}) copy-start(f32[128,128]{1,0:T(8,128)} %copy-done.10) | copy-start | bytes 196612
  1204.1 615.6 %copy-start.13 = (f32[1,128,128]{1,2,0:T(8,128)S(1)}, f32[1,128,128]{1,2,0:T(8,128)}, u32[]{:S(2)}) copy-start(f32[1,128,128]{1,2,0:T(8,128)} %get-tuple-element.212) | copy-start | bytes 196612
  1205.1 172.3 %reduce-scatter.11.cloned.1.call-start = ((), (), s32[]{:S(2)}) async-start(), calls=%async_computation.15 | async-start | bytes 2228224 | tf_op jit(solution)/shard_map/reduce_scatter | solution.py:64
  1205.1 626.2 %copy-start.1 = (f32[256,128]{1,0:T(8,128)S(1)}, f32[256,128]{1,0:T(8,128)}, u32[]{:S(2)}) copy-start(f32[256,128]{1,0:T(8,128)} %param.14) | copy-start | bytes 393220
  1205.7 315.9 %all-reduce.16.cloned.1.call-start = ((), (), s32[]{:S(2)}) async-start(), calls=%async_computation.16 | async-start | bytes 131072 | tf_op jit(solution)/shard_map/psum | solution.py:69
  1379.5 285.0 %all-reduce.18.cloned.1.call-start = ((), (), s32[]{:S(2)}) async-start(), calls=%async_computation.17 | async-start | bytes 262144 | tf_op jit(solution)/shard_map/psum | solution.py:73
  1524.7 280.2 %all-reduce.20.cloned.1.call-start = ((), (), s32[]{:S(2)}) async-start(), calls=%async_computation.18 | async-start | bytes 131072 | tf_op jit(solution)/shard_map/psum | solution.py:75
  (7 other events, 8.2 us)
Sparse Core Ops, SparseCore 0:
  13.3 141.0 all-reduce.7
  180.3 20.8 all-gather.6
  204.1 43.3 all-gather.4
  381.2 94.4 reduce-scatter.4
  479.2 74.2 reduce-scatter.6
  558.7 138.7 all-reduce.9
  703.6 134.6 all-reduce.11
  843.6 134.6 all-reduce.13
  1004.6 20.8 all-gather.10
  1028.3 43.4 all-gather.8
  1205.2 94.4 reduce-scatter.8
  1303.2 74.2 reduce-scatter.10
  1382.8 138.7 all-reduce.15
  1527.5 136.8 all-reduce.17
  1669.6 135.2 all-reduce.19
where the time goes:
time: 1850 us; the launch traced here: 1840 us
  waiting for transfers between devices  1430 us (77%)
  other arithmetic  209 us (11%)
  matrix products  102 us (6%)
  local copies, waits for them, and re-layouts  78.1 us (4%)
    psum x2, waiting for transfers between devices, on_device(): lax.psum(local_gram(current, image_block), ('row', 'col')) / total_rows  284 us
    psum x2, waiting for transfers between devices, on_device(): lax.psum(local_gram(stacked, image_block), ('row', 'col')) / total_rows  278 us
    psum x2, waiting for transfers between devices, on_device(): lax.psum(local_gram(image_block, image_block), ('row', 'col')) / total_rows  275 us
    reduce_scatter x2, waiting for transfers between devices, on_device(): row_sum = lax.psum_scatter(row_part, 'row', scatter_dimension=0, tiled=True)  188 us
    reduce_scatter x2, waiting for transfers between devices, on_device(): col_sum = lax.psum_scatter(col_part, 'col', scatter_dimension=0, tiled=True)  155 us
    psum x1, waiting for transfers between devices, on_device(): lax.psum(local_gram(start_block, start_block), ('row', 'col')) / total_rows  145 us
    all_gather x2, waiting for transfers between devices, on_device(): col_side = lax.all_gather(owned_rows, 'col', axis=0, tiled=True)  83.8 us
    scatter-add x4, other arithmetic, group_step(): col_part.at[cols_now].add(backward)  54 us
  transfers between devices with their start and end apart: 15, of which 14 were waited for; matrix products, arithmetic and copies ran while one was open for 2% of the time, Pallas kernels for 0%

commit v1 on v0

--- a/solution.py
+++ b/solution.py
@@ -1,3 +1,4 @@
+import functools
 import jax
 import jax.numpy as jnp
 from jax import lax
@@ -6,6 +7,16 @@
 BS = 64
 ITERS = 2
 HIGH = lax.Precision.HIGHEST
+
+
+def _resolve_field(u_in, on_dim):
+    return jnp.concatenate(
+        lax.all_to_all(jnp.stack([u_in for _ in range(lax.axis_size("col"))], 0), "col", 0, 0),
+        on_dim,
+    )
+
+
+attach_the_tables = functools.partial(_resolve_field, on_dim=0)
 
 
 def local_gram(left, right):
@@ -35,7 +46,7 @@
     for iteration in range(ITERS):
         owned_rows = current.reshape(owned_blocks, BS, block_width)
         row_side = lax.all_gather(owned_rows, "row", axis=0, tiled=True)
-        col_side = lax.all_gather(owned_rows, "col", axis=0, tiled=True)
+        col_side = attach_the_tables(owned_rows)
         col_length = col_count * owned_blocks
         group_total = (live_count + group_size - 1) // group_size
 

time: 1850 us -> 1780 us (0.962)
  waiting for transfers between devices: 1430 us -> 1360 us
    all_gather x2 -> x0, waiting for transfers between devices: 83.8 us -> none  [on_device(): col_side = lax.all_gather(owned_rows, 'col', axis=0, tiled=True)]
  transfers between devices with their start and end apart: 15 -> 15, of which waited for: 14 -> 13; matrix products, arithmetic and copies ran while one was open for 2% -> 2% of each run, Pallas kernels for 0% -> 0%
where the time goes in v1:
time: 1780 us; the launch traced here: 1770 us
  waiting for transfers between devices  1360 us (76%)
  other arithmetic  209 us (12%)
  matrix products  102 us (6%)
  local copies, waits for them, and re-layouts  80 us (4%)
    psum x2, waiting for transfers between devices, on_device(): lax.psum(local_gram(current, image_block), ('row', 'col')) / total_rows  284 us
    psum x2, waiting for transfers between devices, on_device(): lax.psum(local_gram(stacked, image_block), ('row', 'col')) / total_rows  277 us
    psum x2, waiting for transfers between devices, on_device(): lax.psum(local_gram(image_block, image_block), ('row', 'col')) / total_rows  275 us
    reduce_scatter x2, waiting for transfers between devices, on_device(): row_sum = lax.psum_scatter(row_part, 'row', scatter_dimension=0, tiled=True)  186 us
    reduce_scatter x2, waiting for transfers between devices, on_device(): col_sum = lax.psum_scatter(col_part, 'col', scatter_dimension=0, tiled=True)  155 us
    psum x1, waiting for transfers between devices, on_device(): lax.psum(local_gram(start_block, start_block), ('row', 'col')) / total_rows  145 us
    scatter-add x4, other arithmetic, group_step(): col_part.at[cols_now].add(backward)  54 us
    scatter-add x4, other arithmetic, group_step(): row_part.at[rows_now].add(forward)  54 us
  transfers between devices with their start and end apart: 15, of which 13 were waited for; matrix products, arithmetic and copies ran while one was open for 2% of the time, Pallas kernels for 0%

profile of v1, /device:TPU:1, one launch (start us, length us, event | category | flops | bytes accessed | tf_op | source)
XLA Modules:
  0.0 1771.8 jit_solution(5220066080067109586)
XLA Ops:
  9.1 145.3 %all-reduce.8.cloned.1.call-done = f32[128,128]{0,1:T(8,128)} async-done(((f32[128,128]{0,1:T(8,128)}), f32[128,128]{0,1:T(8,128)}) %all-reduce.8.cloned.1.call-update) | async-done | bytes 65552 | tf_op jit(solution)/shard_map/psum | solution.py:38
  156.2 11.7 cholesky.59
  195.3 20.1 %fusion.27 = s32[384]{0:T(512)S(1)} fusion(s32[384]{0:T(512)S(1)} %copy-done.18, s32[]{:T(128)} %bitcast.7, s32[]{:T(128)} %bitcast.8, s32[]{:T(128)} %bitcast.9, s32[]{:T(128)} %bitcast.10, s32[]{:T(128)} %bitcast.11, s32[]{:T(128)} %bitcast.12, s32[]{:T(128)} %bitcast.13, s32[]{:T(128)} %bitcast.14, s32[]{:T(128)} %bitcast.15, s32[]{:T(128)} %bitcast.16, ...), kind=kLoop, calls=%fused_computation.85 | loop fusion | flops 31104 | bytes 3200 | tf_op jit(solution)/shard_map/add | solution.py:37
  217.1 130.8 %while.24 = (s32[]{:T(128)}, f32[32,64,128]{2,1,0:T(8,128)S(1)}, f32[64,64,128]{2,1,0:T(8,128)}, s32[]{:T(128)}, s32[384]{0:T(512)S(1)}, /*index=5*/f32[384,4096...) while((s32[]{:T(128)}, f32[32,64,128]{2,1,0:T(8,128)S(1)}, ...), condition=%wide.region_6.9_spmd, body=%wide.region_3.0_spmd.sunk | while | flops 1613237376 | bytes 96483616 | solution.py:73
  229.0 12.2 fusion.90
  241.2 13.5 scatter_fusion
  257.5 10.0 fusion.91
  267.6 13.5 scatter_fusion.1
  294.2 12.2 fusion.90
  306.4 13.5 scatter_fusion
  332.7 13.5 scatter_fusion.1
  349.6 93.5 %reduce-scatter.5.cloned.1.call-done = f32[4,64,128]{2,1,0:T(8,128)} async-done(((f32[32,64,128]{2,1,0:T(8,128)}), f32[4,64,128]{2,1,0:T(8,128)}) %reduce-scatter.5.cloned.1.call-update) | async-done | bytes 131088 | tf_op jit(solution)/shard_map/reduce_scatter | solution.py:74
  443.0 77.8 %reduce-scatter.7.cloned.1.call-done = f32[4,64,128]{2,1,0:T(8,128)} async-done(((f32[64,64,128]{2,1,0:T(8,128)}), f32[4,64,128]{2,1,0:T(8,128)}) %reduce-scatter.7.cloned.1.call-update) | async-done | bytes 131088 | tf_op jit(solution)/shard_map/reduce_scatter | solution.py:75
  522.9 141.9 %all-reduce.10.cloned.1.call-done = f32[128,128]{0,1:T(8,128)} async-done(((f32[128,128]{0,1:T(8,128)}), f32[128,128]{0,1:T(8,128)}) %all-reduce.10.cloned.1.call-update) | async-done | bytes 65552 | tf_op jit(solution)/shard_map/psum | solution.py:80
  666.9 138.5 %all-reduce.12.cloned.1.call-done = f32[128,128]{0,1:T(8,128)} async-done(((f32[128,128]{0,1:T(8,128)}), f32[128,128]{0,1:T(8,128)}) %all-reduce.12.cloned.1.call-update) | async-done | bytes 65552 | tf_op jit(solution)/shard_map/psum | solution.py:84
  807.5 137.9 %all-reduce.14.cloned.1.call-done = f32[128,128]{0,1:T(8,128)} async-done(((f32[128,128]{0,1:T(8,128)}), f32[128,128]{0,1:T(8,128)}) %all-reduce.14.cloned.1.call-update) | async-done | bytes 65552 | tf_op jit(solution)/shard_map/psum | solution.py:86
  947.2 11.7 cholesky.70
  977.8 26.5 %all-gather.5.cloned.1.call-done = f32[32,64,128]{2,1,0:T(8,128)} async-done(((f32[4,64,128]{2,1,0:T(8,128)}), f32[32,64,128]{2,1,0:T(8,128)}) %all-gather.5.cloned.1.call-update) | async-done | bytes 1048592 | tf_op jit(solution)/shard_map/all_gather | solution.py:48
  1008.3 130.6 %while.25 = (s32[]{:T(128)}, f32[32,64,128]{2,1,0:T(8,128)S(1)}, f32[64,64,128]{2,1,0:T(8,128)}, s32[]{:T(128)}, s32[384]{0:T(512)S(1)}, /*index=5*/f32[384,4096...) while((s32[]{:T(128)}, f32[32,64,128]{2,1,0:T(8,128)S(1)}, ...), condition=%wide.region_15.18_spmd, body=%wide.region_12.0_spmd.sunk | while | flops 1613237376 | bytes 96483616 | solution.py:73
  1020.2 12.2 fusion.96
  1032.4 13.5 scatter_fusion.2
  1048.7 10.0 fusion.97
  1058.8 13.5 scatter_fusion.3
  1085.4 12.2 fusion.96
  1097.5 13.5 scatter_fusion.2
  1123.9 13.5 scatter_fusion.3
  1140.5 92.7 %reduce-scatter.9.cloned.1.call-done = f32[4,64,128]{2,1,0:T(8,128)} async-done(((f32[32,64,128]{2,1,0:T(8,128)}), f32[4,64,128]{2,1,0:T(8,128)}) %reduce-scatter.9.cloned.1.call-update) | async-done | bytes 131088 | tf_op jit(solution)/shard_map/reduce_scatter | solution.py:74
  1233.3 77.7 %reduce-scatter.11.cloned.1.call-done = f32[4,64,128]{2,1,0:T(8,128)} async-done(((f32[64,64,128]{2,1,0:T(8,128)}), f32[4,64,128]{2,1,0:T(8,128)}) %reduce-scatter.11.cloned.1.call-update) | async-done | bytes 131088 | tf_op jit(solution)/shard_map/reduce_scatter | solution.py:75
  1313.1 142.0 %all-reduce.16.cloned.1.call-done = f32[128,128]{0,1:T(8,128)} async-done(((f32[128,128]{0,1:T(8,128)}), f32[128,128]{0,1:T(8,128)}) %all-reduce.16.cloned.1.call-update) | async-done | bytes 65552 | tf_op jit(solution)/shard_map/psum | solution.py:80
  1459.1 138.9 %all-reduce.18.cloned.1.call-done = f32[256,128]{1,0:T(8,128)} async-done(((f32[256,128]{1,0:T(8,128)}), f32[256,128]{1,0:T(8,128)}) %all-reduce.18.cloned.1.call-update) | async-done | bytes 131088 | tf_op jit(solution)/shard_map/psum | solution.py:84
  1601.0 137.6 %all-reduce.20.cloned.1.call-done = f32[128,128]{0,1:T(8,128)} async-done(((f32[128,128]{0,1:T(8,128)}), f32[128,128]{0,1:T(8,128)}) %all-reduce.20.cloned.1.call-update) | async-done | bytes 65552 | tf_op jit(solution)/shard_map/psum | solution.py:86
  1740.3 11.7 cholesky.81
  (181 shorter events, 173.3 us)
Async XLA Ops:
  7.2 147.2 %all-reduce.8.cloned.1.call-start = ((), (), s32[]{:S(2)}) async-start(), calls=%async_computation.6 | async-start | bytes 131072 | tf_op jit(solution)/shard_map/psum | solution.py:38
  181.1 34.3 %all-to-all-start = ((f32[16,4,64,128]{3,2,1,0:T(8,128)}), f32[16,4,64,128]{3,2,1,0:T(8,128)}, u32[]{:S(2)}, u32[]{:S(2)}) async-start(f32[16,4,64,128]{3,2,1,0:T(8,128)} %stack.24), calls=%async_computation | async-start | bytes 4194304 | tf_op jit(solution)/shard_map/all_to_all | solution.py:14
  185.5 29.8 %all-gather.3.cloned.1.call-start = ((), (), s32[]{:S(2)}) async-start(), calls=%async_computation.7 | async-start | bytes 1179648 | tf_op jit(solution)/shard_map/all_gather | solution.py:48
  186.3 256.7 %reduce-scatter.5.cloned.1.call-start = ((), (), s32[]{:S(2)}) async-start(), calls=%async_computation.8 | async-start | bytes 1179648 | tf_op jit(solution)/shard_map/reduce_scatter | solution.py:74
  187.0 6.6 copy-start.19
  187.0 8.3 copy-start.18
  187.0 30.1 %copy-start.17 = (s32[384]{0:T(512)S(1)}, s32[384]{0:T(512)}, u32[]{:S(2)}) copy-start(s32[384]{0:T(512)} %param.17) | copy-start | bytes 4612
  217.1 304.8 %copy-start.16 = (f32[256]{0:T(256)S(1)}, f32[256]{0:T(256)}, u32[]{:S(2)}) copy-start(f32[256]{0:T(256)} %param.15) | copy-start | bytes 3076
  241.2 13.5 copy-start.4
  257.5 10.0 copy-start.8
  306.4 13.5 copy-start.4
  322.7 10.0 copy-start.8
  348.9 171.9 %reduce-scatter.7.cloned.1.call-start = ((), (), s32[]{:S(2)}) async-start(), calls=%async_computation.9 | async-start | bytes 2228224 | tf_op jit(solution)/shard_map/reduce_scatter | solution.py:75
  349.5 315.3 %all-reduce.10.cloned.1.call-start = ((), (), s32[]{:S(2)}) async-start(), calls=%async_computation.10 | async-start | bytes 131072 | tf_op jit(solution)/shard_map/psum | solution.py:80
  522.8 282.6 %all-reduce.12.cloned.1.call-start = ((), (), s32[]{:S(2)}) async-start(), calls=%async_computation.11 | async-start | bytes 131072 | tf_op jit(solution)/shard_map/psum | solution.py:84
  666.9 278.5 %all-reduce.14.cloned.1.call-start = ((), (), s32[]{:S(2)}) async-start(), calls=%async_computation.12 | async-start | bytes 131072 | tf_op jit(solution)/shard_map/psum | solution.py:86
  958.9 47.7 %copy-start.12 = (f32[128,128]{1,0:T(8,128)}, f32[128,128]{1,0:T(8,128)S(1)}, u32[]{:S(2)}) copy-start(f32[128,128]{1,0:T(8,128)S(1)} %cholesky.70) | copy-start | bytes 196612
  972.6 34.0 %all-to-all-start.1 = ((f32[16,4,64,128]{3,2,1,0:T(8,128)}), f32[16,4,64,128]{3,2,1,0:T(8,128)}, u32[]{:S(2)}, u32[]{:S(2)}) async-start(f32[16,4,64,128]{3,2,1,0:T(8,128)} %stack.26), calls=%async_computation.3 | async-start | bytes 4194304 | tf_op jit(solution)/shard_map/all_to_all | solution.py:14
  977.0 27.3 %all-gather.5.cloned.1.call-start = ((), (), s32[]{:S(2)}) async-start(), calls=%async_computation.13 | async-start | bytes 1179648 | tf_op jit(solution)/shard_map/all_gather | solution.py:48
  977.8 255.5 %reduce-scatter.9.cloned.1.call-start = ((), (), s32[]{:S(2)}) async-start(), calls=%async_computation.14 | async-start | bytes 1179648 | tf_op jit(solution)/shard_map/reduce_scatter | solution.py:74
  1032.4 13.5 copy-start.5
  1048.7 10.0 copy-start.6
  1097.5 13.5 copy-start.5
  1113.8 10.0 copy-start.6
  1138.9 174.1 %copy-start.14 = (f32[128,128]{0,1:T(8,128)S(1)}, f32[128,128]{0,1:T(8,128)}, u32[]{:S(2)}) copy-start(f32[128,128]{0,1:T(8,128)} %all-reduce.10.cloned.1.call-done) | copy-start | bytes 196612
  1138.9 317.3 %copy-start.13 = (f32[128,128]{1,0:T(8,128)S(1)}, f32[128,128]{1,0:T(8,128)}, u32[]{:S(2)}) copy-start(f32[128,128]{1,0:T(8,128)} %copy-done.12) | copy-start | bytes 196612
  1138.9 614.4 %copy-start.15 = (f32[1,128,128]{1,2,0:T(8,128)S(1)}, f32[1,128,128]{1,2,0:T(8,128)}, u32[]{:S(2)}) copy-start(f32[1,128,128]{1,2,0:T(8,128)} %get-tuple-element.212) | copy-start | bytes 196612
  1139.9 171.1 %reduce-scatter.11.cloned.1.call-start = ((), (), s32[]{:S(2)}) async-start(), calls=%async_computation.15 | async-start | bytes 2228224 | tf_op jit(solution)/shard_map/reduce_scatter | solution.py:75
  1140.0 625.1 %copy-start.1 = (f32[256,128]{1,0:T(8,128)S(1)}, f32[256,128]{1,0:T(8,128)}, u32[]{:S(2)}) copy-start(f32[256,128]{1,0:T(8,128)} %param.14) | copy-start | bytes 393220
  1140.5 314.6 %all-reduce.16.cloned.1.call-start = ((), (), s32[]{:S(2)}) async-start(), calls=%async_computation.16 | async-start | bytes 131072 | tf_op jit(solution)/shard_map/psum | solution.py:80
  1313.0 285.0 %all-reduce.18.cloned.1.call-start = ((), (), s32[]{:S(2)}) async-start(), calls=%async_computation.17 | async-start | bytes 262144 | tf_op jit(solution)/shard_map/psum | solution.py:84
  1458.2 280.3 %all-reduce.20.cloned.1.call-start = ((), (), s32[]{:S(2)}) async-start(), calls=%async_computation.18 | async-start | bytes 131072 | tf_op jit(solution)/shard_map/psum | solution.py:86
  (9 other events, 20.4 us)
Sparse Core Ops, SparseCore 0:
  13.3 141.0 all-reduce.7
  188.8 23.9 all-gather.2
  349.1 93.9 reduce-scatter.4
  446.5 74.2 reduce-scatter.6
  526.0 138.7 all-reduce.9
  670.7 134.6 all-reduce.11
  810.7 134.6 all-reduce.13
  980.3 23.9 all-gather.4
  1140.0 93.1 reduce-scatter.8
  1236.7 74.2 reduce-scatter.10
  1316.3 138.7 all-reduce.15
  1461.0 136.8 all-reduce.17
  1603.3 135.2 all-reduce.19
